TPU v7x, 256 devices: a whole 4x4x8 slice. The times are simulated.
256 devices in a mesh: dom: 8 (over z), shard: 32 (over x, y, core).
Axes of the slice: x: 4, y: 4, z: 8, core: 2. Of those that a mesh axis runs over, the one named last changes fastest.
Arguments:
- embedding: float32 [32768, 400], P(('dom', 'shard')), may hold values from -0.9 to 0.9
- accumulator: float32 [32768], P(('dom', 'shard')), may hold values from 0.1 to 1
- relation: float32 [16, 400], replicated, may hold values from 0.1 to 1.9
- plan: int32 [8], replicated, may hold values from 0 to 7, as said below
- lhs_index: int32 [393216], P(('dom', 'shard')), may hold values from 0 to 127
- rhs_index: int32 [393216], P(('dom', 'shard')), may hold values from 0 to 127
- rel_index: int32 [393216], P(('dom', 'shard')), may hold values from 0 to 15
- slot_count: int32 [256, 32], P(('dom', 'shard')), may hold values from 1 to 48, as said below
- neg_span: int32 [768], P(('dom', 'shard')), may hold values from 0 to 2
Outputs:
- entity_grad: float32 [32768, 400], P(('dom', 'shard'))
- adagrad_state: float32 [32768], P(('dom', 'shard'))
- relation_grad: float32 [16, 400], replicated
Inputs may be any that keep to these rules, and one draw needn't show every extreme that they name: plan[d] = d XOR m for one m of 1 to 8 - 1, the same for all d. `slot_count`: every row of groups has some full slot.
All inputs are finite; a program needn't handle non-finite values.
Results may differ from a plain program's by a relative error of at most 0.00079.
Values sent between devices are 32-bit elements; how exact they have to be, the bound alone decides.
No kernel may reach another device: no remote copies, remote signals or barrier semaphores. Data moves between devices by JAX's collectives and lax.ppermute only.
A program may use at most 64 MiB of HBM per device.

v0:
```python
import functools

import jax
import jax.numpy as jnp
from jax import lax
from jax.experimental import pallas as pl
from jax.experimental.pallas import tpu as pltpu
from jax.sharding import PartitionSpec as P

W = 400
R = 128
E = 1536
CH = 512
SLOT = 48
SPANS = 3
N_DOM = 8
N_SHARD = 32
TILE = 256
TILES = E // TILE
SPREAD = 6
FIRST = [TILE * j // SLOT for j in range(TILES)]
PACK = 56
F32 = jnp.float32
BF16 = jnp.bfloat16
NT = (((1,), (1,)), ((), ()))
NN = (((1,), (0,)), ((), ()))


def dot(a, b, dims=NN):
    return lax.dot_general(a, b, dims, preferred_element_type=F32)


def split(x):
    hi = x.astype(BF16)
    return hi, (x - hi.astype(F32)).astype(BF16)


def onehot(mask):
    return jnp.where(mask, 1.0, 0.0).astype(BF16)


def row_at(z_ref, first, index):
    return z_ref[pl.ds(first + index, 1), :]


def rows_of(z_ref, first, j, count=2):
    return jnp.concatenate([row_at(z_ref, first, count * j + i) for i in range(count)], axis=1)


def columns(row):
    return jnp.broadcast_to(row, (R, R)).T


def main_kernel(slot_ref, z_ref, rel_ref, *refs):
    pieces = refs[:10]
    pk_ref, lg_ref, rg_ref = refs[10:13]
    hi_s, lo_s, lhs_s, rel_s, rhs_s, gl_s, gr_s, lhsb_s, rhsb_s, lhsr_s, rhsr_s, bias_s, rows_s, idx_s, rel_acc = refs[13:]

    for side in range(2):
        for piece, places in zip(pieces[5 * side : 5 * side + 5], PLACES):

            def one_table(i, _, piece=piece, first=16 * side + places[0]):
                lanes = pl.ds(pl.multiple_of(slot_ref[first + i] * R, R), R)
                hi, lo = split(piece[i])
                hi_s[:, lanes] = hi
                lo_s[:, lanes] = lo
                return 0

            lax.fori_loop(0, len(places), one_table, 0, unroll=2)

    lt_hi, lt_lo = split(z_ref[:W, :])
    sub_iota = lax.broadcasted_iota(jnp.int32, (SPREAD * R, TILE), 0).astype(F32)
    pad = jnp.zeros((512 - W, TILE), F32)
    rel_iota = lax.broadcasted_iota(jnp.int32, (R, TILE), 0)
    rel_iota = jnp.where(rel_iota < 48, rel_iota % 16, -1).astype(F32)
    rel3 = rel_ref[...]

    def one_tile(j, _):
        c = j // 2
        at = pl.multiple_of((j % 2) * TILE, TILE)
        lanes = pl.ds(at, TILE)
        base = (j * TILE // SLOT) * R
        start = base.astype(F32)
        cols = pl.ds(pl.multiple_of(base, R), SPREAD * R)
        oh = onehot(sub_iota == rows_of(z_ref, W + 12, j) - start)
        hi = hi_s[:, cols]
        rhs = dot(hi, oh) + dot(lo_s[:, cols], oh)
        rhs_s[c, :, lanes] = rhs
        rhsb_s[c, :, lanes] = rhs.astype(BF16)
        named = [columns(row_at(z_ref, W + 12, 2 * j + i)) for i in range(2)]
        rhsr_s[c, lanes, :] = jnp.concatenate([rhs, pad], axis=0).T[:, :W].astype(BF16)
        idx_s[pl.ds(pl.multiple_of(j * TILE, TILE), TILE), :] = jnp.concatenate(named, axis=0)
        oh = onehot(sub_iota[:R] == rows_of(z_ref, W, j))
        lhs = dot(lt_hi, oh) + dot(lt_lo, oh)
        lhs_s[c, :, lanes] = lhs
        lhsb_s[c, :, lanes] = lhs.astype(BF16)
        lhsr_s[c, lanes, :] = jnp.concatenate([lhs, pad], axis=0).T[:, :W].astype(BF16)
        oh = onehot(rel_iota == rows_of(z_ref, W + 24, j))
        rel_s[c, :, lanes] = dot(rel3, oh)
        live = jnp.concatenate([columns(row_at(z_ref, W + 36, 2 * j + i)) for i in range(2)], axis=0)
        bias_s[c, lanes, :] = jnp.where(live > 0.5, 0.0, -jnp.inf)
        return 0

    lax.fori_loop(0, TILES, one_tile, 0, unroll=3)

    gl_s[...] = jnp.zeros_like(gl_s)
    gr_s[...] = jnp.zeros_like(gr_s)
    rel_acc[...] = jnp.zeros_like(rel_acc)
    neg_row = z_ref[W + 48 : W + 49, :]
    lane_row = lax.broadcasted_iota(jnp.int32, (1, R), 1)
    rel_rows = lax.broadcasted_iota(jnp.int32, (16, CH), 0).astype(F32)

    def one_block(c, _):
        n = jnp.sum(jnp.where(lane_row == c, neg_row, 0.0)).astype(jnp.int32)
        lhs, rel, rhs = lhs_s[c], rel_s[c], rhs_s[c]
        left, right = lhs * rel, rhs * rel
        positive = jnp.sum(left * rhs, axis=0, keepdims=True)
        leftb, rightb = left.astype(BF16), right.astype(BF16)
        live = rows_of(z_ref, W + 36, c, 4)
        bias = jnp.concatenate([bias_s[n]] * 4, axis=1)

        def soft(neg_rows, edges):
            scores = dot(neg_rows, edges) + bias
            top = jnp.maximum(positive, jnp.max(scores, axis=0, keepdims=True))
            own = jnp.exp(positive - top)
            others = jnp.exp(scores - top)
            inv = 1.0 / (own + jnp.sum(others, axis=0, keepdims=True))
            return (others * (live * inv)).astype(BF16), own * inv

        tail_w, q_tail = soft(rhsr_s[n], leftb)
        head_w, q_head = soft(lhsr_s[n], rightb)
        weight = live * (q_tail + q_head - 2.0)
        grad_left = weight * rhs + dot(rhsb_s[n], tail_w)
        grad_right = dot(lhsb_s[n], head_w)
        gl_s[c] += grad_left * rel
        gr_s[c] += weight * left + grad_right * rel
        gr_s[n] += dot(leftb, tail_w, NT)
        gl_s[n] += dot(rightb, head_w, NT)
        ghi, glo = split(grad_left * lhs + grad_right * rhs)
        oh = onehot(rel_rows == rows_of(z_ref, W + 24, c, 4))
        rel_acc[...] += dot(oh, ghi, NT) + dot(oh, glo, NT)
        return 0

    lax.fori_loop(0, SPANS, one_block, 0, unroll=1)
    rel_grad = rel_acc[...]
    tail = jnp.concatenate([rel_grad[:, 384:], jnp.zeros((16, R - 16), F32)], axis=1)
    rg_ref[...] = jnp.concatenate([rel_grad[:, :R], rel_grad[:, R : 2 * R], rel_grad[:, 2 * R : 3 * R], tail], axis=0)

    lg_ref[...] = jnp.zeros_like(lg_ref)

    def one_sum(j, _):
        c = j // 2
        lanes = pl.ds(pl.multiple_of((j % 2) * TILE, TILE), TILE)
        oh = onehot(sub_iota[:R] == rows_of(z_ref, W, j))
        hi, lo = split(gl_s[c, :, lanes])
        lg_ref[...] += dot(hi, oh, NT) + dot(lo, oh, NT)
        rows = pl.ds(pl.multiple_of(j * TILE, TILE), TILE)
        rows_s[rows, :] = jnp.concatenate([gr_s[c, :, lanes], pad], axis=0).T
        return 0

    lax.fori_loop(0, TILES, one_sum, 0, unroll=3)
    lane = lax.broadcasted_iota(jnp.int32, (8, R), 1)

    def one_slot(o, _):
        first = pl.multiple_of(o * SLOT, SLOT)
        for k in range(3):
            pk_ref[o, k * SLOT : (k + 1) * SLOT, :] = rows_s[pl.ds(first, SLOT), k * R : (k + 1) * R]
        tail = jnp.zeros((8, R), F32)
        base = (o * R).astype(F32)
        for k in range(SLOT // 8):
            at = pl.ds(pl.multiple_of(first + 8 * k, 8), 8)
            piece = rows_s[at, 3 * R :]
            tail += piece if k == 0 else pltpu.roll(piece, 16 * k, 1)
            tail = jnp.where(lane == 96 + k, idx_s[at, :] - base, tail)
        pk_ref[o, 3 * SLOT :, :] = tail
        return 0

    lax.fori_loop(0, N_SHARD, one_slot, 0, unroll=16)


PLACES = [(0, 1, 2, 3), (4, 5, 6, 7), (12, 13, 14, 15), (8, 9), (10, 11)]
BLOCK = 3 * SLOT + 8


def main_call(slots, z, rel, pieces):
    smem = pl.BlockSpec(memory_space=pltpu.SMEM)
    vmem = pl.BlockSpec(memory_space=pltpu.VMEM)
    big = pltpu.VMEM((SPANS, W, CH), F32)
    half = pltpu.VMEM((SPANS, W, CH), BF16)
    rows = pltpu.VMEM((SPANS, CH, W), BF16)
    return pl.pallas_call(
        main_kernel,
        out_shape=[jax.ShapeDtypeStruct((N_SHARD, BLOCK, R), F32), jax.ShapeDtypeStruct((W, R), F32), jax.ShapeDtypeStruct((64, R), F32)],
        in_specs=[smem] + [vmem] * 12,
        out_specs=[vmem] * 3,
        scratch_shapes=[
            pltpu.VMEM((W, N_SHARD * R), BF16),
            pltpu.VMEM((W, N_SHARD * R), BF16),
            big, big, big, big, big, half, half, rows, rows,
            pltpu.VMEM((SPANS, CH, R), F32),
            pltpu.VMEM((E, 512), F32),
            pltpu.VMEM((E, R), F32),
            pltpu.VMEM((16, W), F32),
        ],
        compiler_params=pltpu.CompilerParams(vmem_limit_bytes=46 * 1024 * 1024),
        cost_estimate=pl.CostEstimate(flops=12_000_000_000, bytes_accessed=14_000_000, transcendentals=1_600_000),
        name="edges",
    )(slots, z, rel, *pieces)


def call(kernel, shapes, name):
    return pl.pallas_call(kernel, out_shape=[jax.ShapeDtypeStruct(v, F32) for v in shapes], name=name)


def pack_kernel(pos_ref, count_ref, neg_ref, table_ref, lhs_ref, rhs_ref, relidx_ref, relation_ref, z_ref, rel_ref, slot_ref):
    x, y, c = pos_ref[0], pos_ref[1], pos_ref[2]
    for side in range(2):
        core = c if side == 0 else 1 - c
        for place in range(16):
            jq, jp = divmod(place, 4)
            dx = jnp.where(core == 0, jp, jq)
            dy = jnp.where(core == 0, jq, jp)
            slot_ref[16 * side + place] = (((x + dx) & 3) * 4 + ((y + dy) & 3)) * 2 + core
    z_ref[:W, :] = table_ref[...]
    shape = (E // R, R)
    edge = lax.broadcasted_iota(jnp.int32, shape, 0) * R + lax.broadcasted_iota(jnp.int32, shape, 1)
    owner = jnp.zeros(shape, jnp.int32)
    live = jnp.zeros(shape, jnp.int32)
    for o in range(N_SHARD):
        inside = jnp.where(edge >= o * SLOT, 1, 0)
        owner = owner + inside
        live = live + inside * jnp.where(edge < o * SLOT + count_ref[0, o], 1, 0) * jnp.where(edge < (o + 1) * SLOT, 1, 0)
    z_ref[W : W + 12, :] = lhs_ref[...].astype(F32)
    z_ref[W + 12 : W + 24, :] = ((owner - 1) * R + rhs_ref[...]).astype(F32)
    z_ref[W + 24 : W + 36, :] = relidx_ref[...].astype(F32)
    z_ref[W + 36 : W + 48, :] = live.astype(F32)
    lane = lax.broadcasted_iota(jnp.int32, (PACK - 48, R), 1)
    neg = jnp.zeros((PACK - 48, R), jnp.int32)
    for c in range(SPANS):
        neg = jnp.where(lane == c, neg_ref[c], neg)
    z_ref[W + 48 :, :] = neg.astype(F32)
    rel = jnp.concatenate([relation_ref[...]] * 8, axis=0)
    rel = jnp.concatenate([rel, jnp.zeros((R, 512 - W), F32)], axis=1).T[:W]
    part = lax.broadcasted_iota(jnp.int32, (W, R), 1) // 16
    hi = rel.astype(BF16).astype(F32)
    mid = (rel - hi).astype(BF16).astype(F32)
    low = rel - hi - mid
    rel_ref[...] = jnp.where(part == 0, hi, jnp.where(part == 1, mid, jnp.where(part == 2, low, 0.0))).astype(BF16)


def pack_call(pos, count, neg, table, lhs, rhs, relidx, relation):
    smem = pl.BlockSpec(memory_space=pltpu.SMEM)
    vmem = pl.BlockSpec(memory_space=pltpu.VMEM)
    return pl.pallas_call(
        pack_kernel,
        out_shape=[
            jax.ShapeDtypeStruct((W + PACK, R), F32),
            jax.ShapeDtypeStruct((W, R), BF16),
            jax.ShapeDtypeStruct((2 * 16,), jnp.int32),
        ],
        in_specs=[smem] * 3 + [vmem] * 5,
        out_specs=[vmem, vmem, smem],
        name="pack",
    )(pos, count, neg, table, lhs, rhs, relidx, relation)


def last_kernel(pk_ref, lhs_ref, acc_ref, ent_ref, state_ref):
    tails = pk_ref[:, 3 * SLOT :, :].reshape(N_SHARD * 8, R)
    names = tails.T
    iota = lax.broadcasted_iota(jnp.int32, (R, N_SHARD * 8), 0).astype(F32)
    lane = lax.broadcasted_iota(jnp.int32, (N_SHARD * 8, R), 1)
    total = jnp.zeros((R, 512), F32)
    for k in range(SLOT // 8):
        oh = onehot(iota == names[96 + k : 97 + k, :])
        tail = tails if k == 0 else pltpu.roll(tails, R - 16 * k, 1)
        blocks = [pk_ref[:, b * SLOT + 8 * k : b * SLOT + 8 * k + 8, :].reshape(N_SHARD * 8, R) for b in range(3)]
        hi, lo = split(jnp.concatenate(blocks + [jnp.where(lane < 16, tail, 0.0)], axis=1))
        total += dot(oh, hi) + dot(oh, lo)
    g = total.T[:W] + lhs_ref[...]
    state_ref[...] = acc_ref[...] + jnp.sum(g * g, axis=0, keepdims=True) * (1.0 / W)
    ent_ref[...] = g


def step_pairs(first, second):
    pairs = []
    for s in range(N_SHARD):
        x, y, c = s // 8, (s // 2) % 4, s % 2
        dx, dy = (first, second) if c == 0 else (second, first)
        pairs.append((s, (((x + dx) % 4) * 4 + (y + dy) % 4) * 2 + c))
    return pairs


def move(value, first=0, second=0):
    return lax.ppermute(value, "shard", step_pairs(first, second))


def swap_core(value):
    return lax.ppermute(value, "shard", [(s, s ^ 1) for s in range(N_SHARD)])


def swap_dom(value, mask):
    return lax.ppermute(value, "dom", [(d, d ^ mask) for d in range(N_DOM)])


def pair_move(value, mask):
    return lax.switch(mask - 1, [functools.partial(swap_dom, mask=m) for m in range(1, N_DOM)], value)


def after(value, first):
    return value + jnp.minimum(jnp.abs(first), 0.0)


def gather_tables(t, pack, mask):
    x1 = jnp.stack([t, move(t, first=-1), move(t, first=2), move(t, first=1)])
    payload, rel, slots = pack(x1[0])
    z = pair_move(payload, mask)
    o1, o3 = move(x1, second=-1), move(x1, second=1)
    f2, g2 = move(after(o3[:2], z[:W]), second=1), move(after(o1[2:], z[:W]), second=-1)
    own = [x1, o1, o3, f2, g2]
    return slots, z, rel, own + [swap_core(v) for v in own]


def sum_shard(value, masks):
    for mask in masks:
        value = value + lax.ppermute(value, "shard", [(s, s ^ mask) for s in range(N_SHARD)])
    return value


def move_back(lhs, rel, mask):
    other = swap_dom(jnp.concatenate([lhs, rel]), mask)
    rel = rel + other[W:]
    for step in {1: (2, 6), 2: (1, 6), 3: (1, 6)}.get(mask, (1, 2)):
        rel = rel + swap_dom(rel, step)
    return other[:W], rel


def local(embedding, accumulator, relation, plan, lhs_index, rhs_index, rel_index, slot_count, neg_span):
    shard = lax.axis_index("shard")
    pos = jnp.stack([shard // 8, (shard // 2) % 4, shard % 2]).astype(jnp.int32)
    mask = plan[0]
    table = embedding.T
    rows = (E // R, R)

    def pack(first):
        indices = [v.reshape(rows) for v in (lhs_index, rhs_index, rel_index)]
        return pack_call(pos, slot_count, neg_span, first, *indices, relation)

    slots, z, rel, pieces = gather_tables(table, pack, mask)
    packed, lhs_grad, rel_grad = main_call(slots, z, rel, pieces)
    returned = lax.all_to_all(packed, "shard", 0, 0, tiled=True)
    back = [functools.partial(move_back, mask=m) for m in range(1, N_DOM)]
    lhs_grad, rel_grad = lax.switch(mask - 1, back, lhs_grad, rel_grad)
    rel_grad = after(sum_shard(rel_grad, (1, 2, 6, 8)), returned[0, :64])
    entity_grad, state = call(last_kernel, [(W, R), (1, R)], "last")(returned, lhs_grad, accumulator.reshape(1, R))
    rel_grad = after(sum_shard(rel_grad, (24,)), entity_grad[:64])
    relation_grad = jnp.concatenate([rel_grad[:16], rel_grad[16:32], rel_grad[32:48], rel_grad[48:, : W - 3 * R]], axis=1)
    return entity_grad.T, state.reshape(R), relation_grad


def solution(mesh):
    both = P(("dom", "shard"))
    rows = P(("dom", "shard"), None)
    in_specs = (rows, both, P(), P(), both, both, both, rows, both)
    return jax.shard_map(local, mesh=mesh, in_specs=in_specs, out_specs=(rows, both, P()), check_vma=False)
```

profile of v0, /device:TPU:24, one launch (start us, length us, event | category | flops | bytes accessed | tf_op | source)
XLA Modules:
  0.0 119.8 jit_solution(5749778612929358193)
XLA Ops:
  0.6 3.1 %collective-permute-start.29 = (f32[400,128]{1,0:T(8,128)}, f32[400,128]{1,0:T(8,128)S(1)}, u32[]{:S(2)}, u32[]{:S(2)}) collective-permute-start(f32[400,128]{1,0:T(8,128)} %bitcast.21), channel_id=1, source_target_pairs={{0,16},{1,5},{2,18},{3,7},{4,20},{5,1},{6,22},{7,3},{8,24},{9,13},... | collective-permute-start | bytes 614408 | tf_op jit(solution)/shard_map/ppermute | solution.py:294
  5.8 2.4 %collective-permute-done.29 = f32[400,128]{1,0:T(8,128)S(1)} collective-permute-done((f32[400,128]{1,0:T(8,128)}, f32[400,128]{1,0:T(8,128)S(1)}, u32[]{:S(2)}, u32[]{:S(2)}) %collective-permute-start.29) | collective-permute-done | bytes 204832 | tf_op jit(solution)/shard_map/ppermute | solution.py:294
  8.2 2.3 %collective-permute-done.28 = f32[400,128]{1,0:T(8,128)S(1)} collective-permute-done((f32[400,128]{1,0:T(8,128)}, f32[400,128]{1,0:T(8,128)S(1)}, u32[]{:S(2)}, u32[]{:S(2)}) %collective-permute-start.28) | collective-permute-done | bytes 204832 | tf_op jit(solution)/shard_map/ppermute | solution.py:294
  10.5 1.6 %collective-permute-done.30 = f32[400,128]{1,0:T(8,128)S(1)} collective-permute-done((f32[400,128]{1,0:T(8,128)}, f32[400,128]{1,0:T(8,128)S(1)}, u32[]{:S(2)}, u32[]{:S(2)}) %collective-permute-start.30) | collective-permute-done | bytes 204832 | tf_op jit(solution)/shard_map/ppermute | solution.py:294
  13.4 1.7 %collective-permute-start.31 = (f32[4,400,128]{2,1,0:T(8,128)S(1)}, f32[4,400,128]{2,1,0:T(8,128)S(1)}, u32[]{:S(2)}, u32[]{:S(2)}) collective-permute-start(f32[4,400,128]{2,1,0:T(8,128)S(1)} %pad_maximum_fusion.7.refs_0_), channel_id=1, source_target_pairs={{0,6},{1,25},{2,0},{3,27},{4,2},{5,29},{6,4},{7,31},{8,14},{9,1},{... | collective-permute-start | bytes 2457608 | tf_op jit(solution)/shard_map/ppermute | solution.py:294
  16.5 1.8 %pack.1 = (f32[456,128]{1,0:T(8,128)S(1)}, bf16[400,128]{1,0:T(8,128)(2,1)}, s32[32]{0:T(128)}) custom-call(s32[3]{0:T(128)} %pad_add_fusion.pos_ref, s32[1,32]{1,0:T(1,128)} %count_ref.1, s32[3]{0:T(128)} %neg_ref.1, f32[400,128]{1,0:T(8,128)} %bitcast.25, s32[12,128]{1,0:T(8,128)} %bitcast.29, s32[12,128]{1,0:T(8,128)} %bitcast.30, s32[12,128]{1,0:T(8,128)} %bitcast.31, ...), custom_call_target="tpu_custom_call" | custom-call | tf_op jit(solution)/shard_map/pack/pallas_call | solution.py:254
  18.2 14.9 %conditional.2 = (f32[456,128]{1,0:T(8,128)}) conditional(s32[]{:T(128)} %bitcast.7, f32[456,128]{1,0:T(8,128)S(1)} %get-tuple-element.81, f32[456,128]{1,0:T(8,128)S(1)} %get-tuple-element.81, f32[456,128]{1,0:T(8,128)S(1)} %get-tuple-element.81, f32[456,128]{1,0:T(8,128)S(1)} %get-tuple-element.81, ...), branch_computations={%region_0.1_spmd, %region_1.2_spmd, %region_2.3_spmd, %region_3.4_... | conditional | bytes 933936 | solution.py:306
  18.3 7.3 %collective-permute-start.3 = (f32[456,128]{1,0:T(8,128)S(1)}, f32[456,128]{1,0:T(8,128)}, u32[]{:S(2)}, u32[]{:S(2)}) collective-permute-start(f32[456,128]{1,0:T(8,128)S(1)} %param.3), channel_id=1, source_target_pairs={{0,128},{32,160},{64,192},{96,224},{128,0},{160,32},{192,64},{224,... | collective-permute-start | bytes 700424 | tf_op jit(solution)/shard_map/cond/branch_3_fun/ppermute | solution.py:302
  25.5 7.6 %collective-permute-done.3 = f32[456,128]{1,0:T(8,128)} collective-permute-done((f32[456,128]{1,0:T(8,128)S(1)}, f32[456,128]{1,0:T(8,128)}, u32[]{:S(2)}, u32[]{:S(2)}) %collective-permute-start.3) | collective-permute-done | bytes 233504 | tf_op jit(solution)/shard_map/cond/branch_3_fun/ppermute | solution.py:302
  35.3 2.4 %collective-permute-start.33 = (f32[2,400,128]{2,1,0:T(8,128)S(1)}, f32[2,400,128]{2,1,0:T(8,128)S(1)}, u32[]{:S(2)}, u32[]{:S(2)}) collective-permute-start(f32[2,400,128]{2,1,0:T(8,128)S(1)} %get-tuple-element.92), channel_id=1, source_target_pairs={{0,2},{1,9},{2,4},{3,11},{4,6},{5,13},{6,0},{7,15},{8,10},{9,17},{... | collective-permute-start | bytes 1228808 | tf_op jit(solution)/shard_map/ppermute | solution.py:294
  37.6 5.9 %collective-permute-done.34.refs_4_ = f32[2,400,128]{2,1,0:T(8,128)S(1)} collective-permute-done((f32[2,400,128]{2,1,0:T(8,128)S(1)}, f32[2,400,128]{2,1,0:T(8,128)S(1)}, u32[]{:S(2)}, u32[]{:S(2)}) %collective-permute-start.34) | collective-permute-done | bytes 409632 | tf_op jit(solution)/shard_map/ppermute | solution.py:294
  47.5 16.6 %edges.1 = (f32[32,152,128]{2,1,0:T(8,128)}, f32[400,128]{1,0:T(8,128)S(1)}, f32[64,128]{1,0:T(8,128)S(1)}) custom-call(s32[32]{0:T(128)S(1)} %copy-done.1, f32[456,128]{1,0:T(8,128)} %get-tuple-element.152.z_ref, bf16[400,128]{1,0:T(8,128)(2,1)S(1)} %copy-done, f32[4,400,128]{2,1,0:T(8,128)S(1)} %pad_maximum_fusion.7.refs_0_, ...), custom_call_target="tpu_custom_call" | custom-call | flops 12000000000 | bytes 14000000 | tf_op jit(solution)/shard_map/edges/pallas_call | solution.py:191
  64.1 6.4 %all-to-all-start = ((f32[32,152,128]{2,1,0:T(8,128)}), f32[32,152,128]{2,1,0:T(8,128)S(1)}, u32[]{:S(2)}, u32[]{:S(2)}) async-start(f32[32,152,128]{2,1,0:T(8,128)} %get-tuple-element.83), calls=%async_computation | async-start | bytes 4980736 | tf_op jit(solution)/shard_map/all_to_all | solution.py:350
  70.5 26.9 %conditional.3 = (f32[64,128]{1,0:T(8,128)}, f32[64,128]{1,0:T(8,128)S(1)}, f32[64,128]{1,0:T(8,128)}, f32[400,128]{1,0:T(8,128)S(1)}) conditional(s32[]{:T(128)} %bitcast.7, (f32[400,128]{1,0:T(8,128)S(1)}, f32[64,128]{1,0:T(8,128)S(1)}) %tuple.102, (f32[400,128]{1,0:T(8,128)S(1)}, ...), branch_computations={%region_7.8_spmd, %region_8.9_spmd, %region_9.10_spmd, %region_10.... | conditional | flops 75776 | bytes 2359448 | solution.py:352
  70.5 6.5 %collective-permute-start.16 = (f32[464,128]{1,0:T(8,128)S(1)}, f32[464,128]{1,0:T(8,128)S(1)}, u32[]{:S(2)}, u32[]{:S(2)}) collective-permute-start(f32[464,128]{1,0:T(8,128)S(1)} %pad_maximum_fusion.3), channel_id=1, source_target_pairs={{0,128},{32,160},{64,192},{96,224},{128,0},{160,32},{192,64},{224,... | collective-permute-start | bytes 712712 | tf_op jit(solution)/shard_map/cond/branch_3_fun/ppermute | solution.py:302
  77.1 7.1 %collective-permute-done.16 = f32[464,128]{1,0:T(8,128)S(1)} collective-permute-done((f32[464,128]{1,0:T(8,128)S(1)}, f32[464,128]{1,0:T(8,128)S(1)}, u32[]{:S(2)}, u32[]{:S(2)}) %collective-permute-start.16) | collective-permute-done | bytes 237600 | tf_op jit(solution)/shard_map/cond/branch_3_fun/ppermute | solution.py:302
  84.2 5.1 %collective-permute-start.17 = (f32[64,128]{1,0:T(8,128)S(1)}, f32[64,128]{1,0:T(8,128)S(1)}, u32[]{:S(2)}, u32[]{:S(2)}) collective-permute-start(f32[64,128]{1,0:T(8,128)S(1)} %slice_add_fusion.3), channel_id=1, source_target_pairs={{0,32},{32,0},{64,96},{96,64},{128,160},{160,128},{192,224},{224,1... | collective-permute-start | bytes 98312 | tf_op jit(solution)/shard_map/cond/branch_3_fun/ppermute | solution.py:302
  89.3 1.9 %collective-permute-done.17 = f32[64,128]{1,0:T(8,128)S(1)} collective-permute-done((f32[64,128]{1,0:T(8,128)S(1)}, f32[64,128]{1,0:T(8,128)S(1)}, u32[]{:S(2)}, u32[]{:S(2)}) %collective-permute-start.17) | collective-permute-done | bytes 32800 | tf_op jit(solution)/shard_map/cond/branch_3_fun/ppermute | solution.py:302
  91.8 3.4 %collective-permute-start.18 = (f32[64,128]{1,0:T(8,128)}, f32[64,128]{1,0:T(8,128)}, u32[]{:S(2)}, u32[]{:S(2)}) collective-permute-start(f32[64,128]{1,0:T(8,128)} %add.78), channel_id=1, source_target_pairs={{0,64},{32,96},{64,0},{96,32},{128,192},{160,224},{192,128},{224,1... | collective-permute-start | bytes 98312 | tf_op jit(solution)/shard_map/cond/branch_3_fun/ppermute | solution.py:302
  100.2 3.1 %collective-permute-done.41 = f32[64,128]{1,0:T(8,128)S(1)} collective-permute-done((f32[64,128]{1,0:T(8,128)S(1)}, f32[64,128]{1,0:T(8,128)S(1)}, u32[]{:S(2)}, u32[]{:S(2)}) %collective-permute-start.41) | collective-permute-done | bytes 32800 | tf_op jit(solution)/shard_map/ppermute | solution.py:325
  103.6 4.8 %collective-permute-done.42 = f32[64,128]{1,0:T(8,128)S(1)} collective-permute-done((f32[64,128]{1,0:T(8,128)S(1)}, f32[64,128]{1,0:T(8,128)S(1)}, u32[]{:S(2)}, u32[]{:S(2)}) %collective-permute-start.42) | collective-permute-done | bytes 32800 | tf_op jit(solution)/shard_map/ppermute | solution.py:325
  109.9 2.4 %collective-permute-done.43 = f32[64,128]{1,0:T(8,128)S(1)} collective-permute-done((f32[64,128]{1,0:T(8,128)S(1)}, f32[64,128]{1,0:T(8,128)S(1)}, u32[]{:S(2)}, u32[]{:S(2)}) %collective-permute-start.43) | collective-permute-done | bytes 32800 | tf_op jit(solution)/shard_map/ppermute | solution.py:325
  112.3 2.9 %collective-permute-start.44 = (f32[64,128]{1,0:T(8,128)S(1)}, f32[64,128]{1,0:T(8,128)S(1)}, u32[]{:S(2)}, u32[]{:S(2)}) collective-permute-start(f32[64,128]{1,0:T(8,128)S(1)} %fusion.3), channel_id=1, source_target_pairs={{0,24},{1,25},{2,26},{3,27},{4,28},{5,29},{6,30},{7,31},{8,16},{9,... | collective-permute-start | bytes 98312 | tf_op jit(solution)/shard_map/ppermute | solution.py:325
  115.2 3.2 %last.1 = (f32[400,128]{1,0:T(8,128)}, f32[1,128]{1,0:T(1,128)}) custom-call(f32[32,152,128]{2,1,0:T(8,128)} %copy-done.2, f32[400,128]{1,0:T(8,128)S(1)} %get-tuple-element.86.lhs_ref, f32[1,128]{1,0:T(1,128)} %bitcast.33), custom_call_target="tpu_custom_call" | custom-call | tf_op jit(solution)/shard_map/last/pallas_call | solution.py:354
  (49 shorter events, 18.9 us)
Async XLA Ops:
  0.6 7.6 %collective-permute-start.29 = (f32[400,128]{1,0:T(8,128)}, f32[400,128]{1,0:T(8,128)S(1)}, u32[]{:S(2)}, u32[]{:S(2)}) collective-permute-start(f32[400,128]{1,0:T(8,128)} %bitcast.21), channel_id=1, source_target_pairs={{0,16},{1,5},{2,18},{3,7},{4,20},{5,1},{6,22},{7,3},{8,24},{9,13},... | collective-permute-start | bytes 614408 | tf_op jit(solution)/shard_map/ppermute | solution.py:294
  3.7 6.7 %collective-permute-start.28 = (f32[400,128]{1,0:T(8,128)}, f32[400,128]{1,0:T(8,128)S(1)}, u32[]{:S(2)}, u32[]{:S(2)}) collective-permute-start(f32[400,128]{1,0:T(8,128)} %bitcast.22), channel_id=1, source_target_pairs={{0,24},{1,7},{2,26},{3,1},{4,28},{5,3},{6,30},{7,5},{8,0},{9,15},{... | collective-permute-start | bytes 614408 | tf_op jit(solution)/shard_map/ppermute | solution.py:294
  4.9 7.2 %collective-permute-start.30 = (f32[400,128]{1,0:T(8,128)}, f32[400,128]{1,0:T(8,128)S(1)}, u32[]{:S(2)}, u32[]{:S(2)}) collective-permute-start(f32[400,128]{1,0:T(8,128)} %bitcast.23), channel_id=1, source_target_pairs={{0,8},{1,3},{2,10},{3,5},{4,12},{5,7},{6,14},{7,1},{8,16},{9,11},{... | collective-permute-start | bytes 614408 | tf_op jit(solution)/shard_map/ppermute | solution.py:294
  13.0 21.2 %collective-permute-start.32 = (f32[4,400,128]{2,1,0:T(8,128)S(1)}, f32[4,400,128]{2,1,0:T(8,128)S(1)}, u32[]{:S(2)}, u32[]{:S(2)}) collective-permute-start(f32[4,400,128]{2,1,0:T(8,128)S(1)} %pad_maximum_fusion.7.refs_0_), channel_id=1, source_target_pairs={{0,2},{1,9},{2,4},{3,11},{4,6},{5,13},{6,0},{7,15},{8,10},{9,17},{... | collective-permute-start | bytes 2457608 | tf_op jit(solution)/shard_map/ppermute | solution.py:294
  13.4 20.8 %collective-permute-start.31 = (f32[4,400,128]{2,1,0:T(8,128)S(1)}, f32[4,400,128]{2,1,0:T(8,128)S(1)}, u32[]{:S(2)}, u32[]{:S(2)}) collective-permute-start(f32[4,400,128]{2,1,0:T(8,128)S(1)} %pad_maximum_fusion.7.refs_0_), channel_id=1, source_target_pairs={{0,6},{1,25},{2,0},{3,27},{4,2},{5,29},{6,4},{7,31},{8,14},{9,1},{... | collective-permute-start | bytes 2457608 | tf_op jit(solution)/shard_map/ppermute | solution.py:294
  18.3 14.9 %collective-permute-start.3 = (f32[456,128]{1,0:T(8,128)S(1)}, f32[456,128]{1,0:T(8,128)}, u32[]{:S(2)}, u32[]{:S(2)}) collective-permute-start(f32[456,128]{1,0:T(8,128)S(1)} %param.3), channel_id=1, source_target_pairs={{0,128},{32,160},{64,192},{96,224},{128,0},{160,32},{192,64},{224,... | collective-permute-start | bytes 700424 | tf_op jit(solution)/shard_map/cond/branch_3_fun/ppermute | solution.py:302
  34.1 10.0 %collective-permute-start.35 = (f32[4,400,128]{2,1,0:T(8,128)S(1)}, f32[4,400,128]{2,1,0:T(8,128)S(1)}, u32[]{:S(2)}, u32[]{:S(2)}) collective-permute-start(f32[4,400,128]{2,1,0:T(8,128)S(1)} %pad_maximum_fusion.7.refs_0_), channel_id=1, source_target_pairs={{0,1},{1,0},{2,3},{3,2},{4,5},{5,4},{6,7},{7,6},{8,9},{9,8},{10,11... | collective-permute-start | bytes 2457608 | tf_op jit(solution)/shard_map/ppermute | solution.py:298
  34.3 9.2 %collective-permute-start.34 = (f32[2,400,128]{2,1,0:T(8,128)S(1)}, f32[2,400,128]{2,1,0:T(8,128)S(1)}, u32[]{:S(2)}, u32[]{:S(2)}) collective-permute-start(f32[2,400,128]{2,1,0:T(8,128)S(1)} %get-tuple-element.91), channel_id=1, source_target_pairs={{0,6},{1,25},{2,0},{3,27},{4,2},{5,29},{6,4},{7,31},{8,14},{9,1},{... | collective-permute-start | bytes 1228808 | tf_op jit(solution)/shard_map/ppermute | solution.py:294
  35.3 8.8 %collective-permute-start.37 = (f32[4,400,128]{2,1,0:T(8,128)S(1)}, f32[4,400,128]{2,1,0:T(8,128)S(1)}, u32[]{:S(2)}, u32[]{:S(2)}) collective-permute-start(f32[4,400,128]{2,1,0:T(8,128)S(1)} %collective-permute-done.32.refs_2_), channel_id=1, source_target_pairs={{0,1},{1,0},{2,3},{3,2},{4,5},{5,4},{6,7},{7,6},{8,9},{9,8},{10,11... | collective-permute-start | bytes 2457608 | tf_op jit(solution)/shard_map/ppermute | solution.py:298
  35.3 8.3 %collective-permute-start.33 = (f32[2,400,128]{2,1,0:T(8,128)S(1)}, f32[2,400,128]{2,1,0:T(8,128)S(1)}, u32[]{:S(2)}, u32[]{:S(2)}) collective-permute-start(f32[2,400,128]{2,1,0:T(8,128)S(1)} %get-tuple-element.92), channel_id=1, source_target_pairs={{0,2},{1,9},{2,4},{3,11},{4,6},{5,13},{6,0},{7,15},{8,10},{9,17},{... | collective-permute-start | bytes 1228808 | tf_op jit(solution)/shard_map/ppermute | solution.py:294
  37.6 8.3 %collective-permute-start.36 = (f32[4,400,128]{2,1,0:T(8,128)S(1)}, f32[4,400,128]{2,1,0:T(8,128)S(1)}, u32[]{:S(2)}, u32[]{:S(2)}) collective-permute-start(f32[4,400,128]{2,1,0:T(8,128)S(1)} %collective-permute-done.31.refs_1_), channel_id=1, source_target_pairs={{0,1},{1,0},{2,3},{3,2},{4,5},{5,4},{6,7},{7,6},{8,9},{9,8},{10,11... | collective-permute-start | bytes 2457608 | tf_op jit(solution)/shard_map/ppermute | solution.py:298
  43.6 1.7 %collective-permute-start.39 = (f32[2,400,128]{2,1,0:T(8,128)S(1)}, f32[2,400,128]{2,1,0:T(8,128)S(1)}, u32[]{:S(2)}, u32[]{:S(2)}) collective-permute-start(f32[2,400,128]{2,1,0:T(8,128)S(1)} %collective-permute-done.34.refs_4_), channel_id=1, source_target_pairs={{0,1},{1,0},{2,3},{3,2},{4,5},{5,4},{6,7},{7,6},{8,9},{9,8},{10,11... | collective-permute-start | bytes 1228808 | tf_op jit(solution)/shard_map/ppermute | solution.py:298
  43.6 2.3 %collective-permute-start.38 = (f32[2,400,128]{2,1,0:T(8,128)S(1)}, f32[2,400,128]{2,1,0:T(8,128)S(1)}, u32[]{:S(2)}, u32[]{:S(2)}) collective-permute-start(f32[2,400,128]{2,1,0:T(8,128)S(1)} %collective-permute-done.33.refs_3_), channel_id=1, source_target_pairs={{0,1},{1,0},{2,3},{3,2},{4,5},{5,4},{6,7},{7,6},{8,9},{9,8},{10,11... | collective-permute-start | bytes 1228808 | tf_op jit(solution)/shard_map/ppermute | solution.py:298
  45.9 0.9 copy-start
  64.1 48.2 %all-to-all-start = ((f32[32,152,128]{2,1,0:T(8,128)}), f32[32,152,128]{2,1,0:T(8,128)S(1)}, u32[]{:S(2)}, u32[]{:S(2)}) async-start(f32[32,152,128]{2,1,0:T(8,128)} %get-tuple-element.83), calls=%async_computation | async-start | bytes 4980736 | tf_op jit(solution)/shard_map/all_to_all | solution.py:350
  70.5 13.7 %collective-permute-start.16 = (f32[464,128]{1,0:T(8,128)S(1)}, f32[464,128]{1,0:T(8,128)S(1)}, u32[]{:S(2)}, u32[]{:S(2)}) collective-permute-start(f32[464,128]{1,0:T(8,128)S(1)} %pad_maximum_fusion.3), channel_id=1, source_target_pairs={{0,128},{32,160},{64,192},{96,224},{128,0},{160,32},{192,64},{224,... | collective-permute-start | bytes 712712 | tf_op jit(solution)/shard_map/cond/branch_3_fun/ppermute | solution.py:302
  84.2 7.0 %collective-permute-start.17 = (f32[64,128]{1,0:T(8,128)S(1)}, f32[64,128]{1,0:T(8,128)S(1)}, u32[]{:S(2)}, u32[]{:S(2)}) collective-permute-start(f32[64,128]{1,0:T(8,128)S(1)} %slice_add_fusion.3), channel_id=1, source_target_pairs={{0,32},{32,0},{64,96},{96,64},{128,160},{160,128},{192,224},{224,1... | collective-permute-start | bytes 98312 | tf_op jit(solution)/shard_map/cond/branch_3_fun/ppermute | solution.py:302
  91.8 5.6 %collective-permute-start.18 = (f32[64,128]{1,0:T(8,128)}, f32[64,128]{1,0:T(8,128)}, u32[]{:S(2)}, u32[]{:S(2)}) collective-permute-start(f32[64,128]{1,0:T(8,128)} %add.78), channel_id=1, source_target_pairs={{0,64},{32,96},{64,0},{96,32},{128,192},{160,224},{192,128},{224,1... | collective-permute-start | bytes 98312 | tf_op jit(solution)/shard_map/cond/branch_3_fun/ppermute | solution.py:302
  98.1 1.2 %collective-permute-start.40 = (f32[64,128]{1,0:T(8,128)S(1)}, f32[64,128]{1,0:T(8,128)S(1)}, u32[]{:S(2)}, u32[]{:S(2)}) collective-permute-start(f32[64,128]{1,0:T(8,128)S(1)} %add.103), channel_id=1, source_target_pairs={{0,1},{1,0},{2,3},{3,2},{4,5},{5,4},{6,7},{7,6},{8,9},{9,8},{10,11... | collective-permute-start | bytes 98312 | tf_op jit(solution)/shard_map/ppermute | solution.py:325
  99.3 3.9 %collective-permute-start.41 = (f32[64,128]{1,0:T(8,128)S(1)}, f32[64,128]{1,0:T(8,128)S(1)}, u32[]{:S(2)}, u32[]{:S(2)}) collective-permute-start(f32[64,128]{1,0:T(8,128)S(1)} %add.104), channel_id=1, source_target_pairs={{0,2},{1,3},{2,0},{3,1},{4,6},{5,7},{6,4},{7,5},{8,10},{9,11},{10,... | collective-permute-start | bytes 98312 | tf_op jit(solution)/shard_map/ppermute | solution.py:325
  103.2 5.1 %collective-permute-start.42 = (f32[64,128]{1,0:T(8,128)S(1)}, f32[64,128]{1,0:T(8,128)S(1)}, u32[]{:S(2)}, u32[]{:S(2)}) collective-permute-start(f32[64,128]{1,0:T(8,128)S(1)} %add.105), channel_id=1, source_target_pairs={{0,6},{1,7},{2,4},{3,5},{4,2},{5,3},{6,0},{7,1},{8,14},{9,15},{10,... | collective-permute-start | bytes 98312 | tf_op jit(solution)/shard_map/ppermute | solution.py:325
  108.4 3.9 %collective-permute-start.43 = (f32[64,128]{1,0:T(8,128)S(1)}, f32[64,128]{1,0:T(8,128)S(1)}, u32[]{:S(2)}, u32[]{:S(2)}) collective-permute-start(f32[64,128]{1,0:T(8,128)S(1)} %add.106), channel_id=1, source_target_pairs={{0,8},{1,9},{2,10},{3,11},{4,12},{5,13},{6,14},{7,15},{8,0},{9,1},... | collective-permute-start | bytes 98312 | tf_op jit(solution)/shard_map/ppermute | solution.py:325
  112.3 2.9 %copy-start.2 = (f32[32,152,128]{2,1,0:T(8,128)}, f32[32,152,128]{2,1,0:T(8,128)S(1)}, u32[]{:S(2)}) copy-start(f32[32,152,128]{2,1,0:T(8,128)S(1)} %all-to-all-done.pk_ref) | copy-start | bytes 7471108
  112.3 6.1 %collective-permute-start.44 = (f32[64,128]{1,0:T(8,128)S(1)}, f32[64,128]{1,0:T(8,128)S(1)}, u32[]{:S(2)}, u32[]{:S(2)}) collective-permute-start(f32[64,128]{1,0:T(8,128)S(1)} %fusion.3), channel_id=1, source_target_pairs={{0,24},{1,25},{2,26},{3,27},{4,28},{5,29},{6,30},{7,31},{8,16},{9,... | collective-permute-start | bytes 98312 | tf_op jit(solution)/shard_map/ppermute | solution.py:325
  (1 other events, 0.7 us)
where the time goes:
time: 120 us
  starting transfers between devices  45.4 us (38%)
  waiting for transfers between devices  43.6 us (36%)
  Pallas kernels  21.5 us (18%)
  other arithmetic  5.47 us (5%)
  local copies, waits for them, and re-layouts  2.35 us (2%)
  between operations  1.39 us (1%)
    ppermute x4, starting transfers between devices, swap_dom(): return lax.ppermute(value, 'dom', [(d, d ^ mask) for d in range(N_DOM)])  22.3 us
    ppermute x4, waiting for transfers between devices, swap_dom(): return lax.ppermute(value, 'dom', [(d, d ^ mask) for d in range(N_DOM)])  18.1 us
    pallas_call x1, Pallas kernels, main_call(): pl.pallas_call(main_kernel, out_shape=[jax.ShapeDtypeStruct((N_SHARD, BLO...  16.6 us
    ppermute x7, waiting for transfers between devices, move(): return lax.ppermute(value, 'shard', step_pairs(first, second))  12.2 us
    ppermute x5, waiting for transfers between devices, sum_shard(): lax.ppermute(value, 'shard', [(s, s ^ mask) for s in range(N_SHARD)])  11.5 us
    ppermute x7, starting transfers between devices, move(): return lax.ppermute(value, 'shard', step_pairs(first, second))  10.6 us
    all_to_all x1, starting transfers between devices, local(): returned = lax.all_to_all(packed, 'shard', 0, 0, tiled=True)  6.4 us
    ppermute x5, starting transfers between devices, sum_shard(): lax.ppermute(value, 'shard', [(s, s ^ mask) for s in range(N_SHARD)])  5.61 us
  transfers between devices with their start and end apart: 22, of which 14 were waited for; matrix products, arithmetic and copies ran while one was open for 3% of the time, Pallas kernels for 4%

commit v1 on v0

--- a/solution.py
+++ b/solution.py
@@ -276,7 +276,7 @@
         blocks = [pk_ref[:, b * SLOT + 8 * k : b * SLOT + 8 * k + 8, :].reshape(N_SHARD * 8, R) for b in range(3)]
         hi, lo = split(jnp.concatenate(blocks + [jnp.where(lane < 16, tail, 0.0)], axis=1))
         total += dot(oh, hi) + dot(oh, lo)
-    g = total.T[:W] + lhs_ref[...]
+    g = total.T[:W] + lhs_ref[:W, :]
     state_ref[...] = acc_ref[...] + jnp.sum(g * g, axis=0, keepdims=True) * (1.0 / W)
     ent_ref[...] = g
 
@@ -311,8 +311,8 @@
 
 
 def gather_tables(t, pack, mask):
-    x1 = jnp.stack([t, move(t, first=-1), move(t, first=2), move(t, first=1)])
-    payload, rel, slots = pack(x1[0])
+    payload, rel, slots = pack(t)
+    x1 = jnp.stack([payload[:W], move(t, first=-1), move(t, first=2), move(t, first=1)])
     z = pair_move(payload, mask)
     o1, o3 = move(x1, second=-1), move(x1, second=1)
     f2, g2 = move(after(o3[:2], z[:W]), second=1), move(after(o1[2:], z[:W]), second=-1)
@@ -331,7 +331,7 @@
     rel = rel + other[W:]
     for step in {1: (2, 6), 2: (1, 6), 3: (1, 6)}.get(mask, (1, 2)):
         rel = rel + swap_dom(rel, step)
-    return other[:W], rel
+    return other, rel
 
 
 def local(embedding, accumulator, relation, plan, lhs_index, rhs_index, rel_index, slot_count, neg_span):

time: 120 us -> 113 us (0.942)
  starting transfers between devices: 45.4 us -> 30.1 us
  waiting for transfers between devices: 43.6 us -> 52.6 us
  local copies, waits for them, and re-layouts: 2.35 us -> 0.83 us
    ppermute x4, starting transfers between devices: 22.3 us -> 9.42 us  [swap_dom(): return lax.ppermute(value, 'dom', [(d, d ^ mask) for d in range(N_DOM)])]
    ppermute x4, waiting for transfers between devices: 18.1 us -> 27.2 us  [swap_dom(): return lax.ppermute(value, 'dom', [(d, d ^ mask) for d in range(N_DOM)])]
    ppermute x7, waiting for transfers between devices: 12.2 us -> 8.68 us  [move(): return lax.ppermute(value, 'shard', step_pairs(first, second))]
    ppermute x5, waiting for transfers between devices: 11.5 us -> 15 us  [sum_shard(): lax.ppermute(value, 'shard', [(s, s ^ mask) for s in range(N_SHARD)])]
    ppermute x5, starting transfers between devices: 5.61 us -> 2.95 us  [sum_shard(): lax.ppermute(value, 'shard', [(s, s ^ mask) for s in range(N_SHARD)])]
    unnamed x6, local copies, waits for them, and re-layouts: 1.55 us -> 0.02 us
  transfers between devices with their start and end apart: 22 -> 22, of which waited for: 14 -> 14; matrix products, arithmetic and copies ran while one was open for 3% -> 4% of each run, Pallas kernels for 4% -> 5%
where the time goes in v1:
time: 113 us; the launch traced here: 112 us
  waiting for transfers between devices  52.6 us (47%)
  starting transfers between devices  30.1 us (27%)
  Pallas kernels  21.7 us (19%)
  other arithmetic  5.3 us (5%)
  between operations  1.43 us (1%)
    ppermute x4, waiting for transfers between devices, swap_dom(): return lax.ppermute(value, 'dom', [(d, d ^ mask) for d in range(N_DOM)])  27.2 us
    pallas_call x1, Pallas kernels, main_call(): pl.pallas_call(main_kernel, out_shape=[jax.ShapeDtypeStruct((N_SHARD, BLO...  16.6 us
    ppermute x5, waiting for transfers between devices, sum_shard(): lax.ppermute(value, 'shard', [(s, s ^ mask) for s in range(N_SHARD)])  15 us
    ppermute x7, starting transfers between devices, move(): return lax.ppermute(value, 'shard', step_pairs(first, second))  10.4 us
    ppermute x4, starting transfers between devices, swap_dom(): return lax.ppermute(value, 'dom', [(d, d ^ mask) for d in range(N_DOM)])  9.42 us
    ppermute x7, waiting for transfers between devices, move(): return lax.ppermute(value, 'shard', step_pairs(first, second))  8.68 us
    all_to_all x1, starting transfers between devices, local(): returned = lax.all_to_all(packed, 'shard', 0, 0, tiled=True)  6.4 us
    pallas_call x1, Pallas kernels, local(): call(last_kernel, [(W, R), (1, R)], 'last')  3.31 us
  transfers between devices with their start and end apart: 22, of which 14 were waited for; matrix products, arithmetic and copies ran while one was open for 4% of the time, Pallas kernels for 5%

profile of v1, /device:TPU:24, one launch (start us, length us, event | category | flops | bytes accessed | tf_op | source)
XLA Modules:
  0.0 112.0 jit_solution(12815164554852479682)
XLA Ops:
  0.6 1.6 %collective-permute-start.30 = (f32[400,128]{1,0:T(8,128)}, f32[400,128]{1,0:T(8,128)S(1)}, u32[]{:S(2)}, u32[]{:S(2)}) collective-permute-start(f32[400,128]{1,0:T(8,128)} %bitcast.24), channel_id=1, source_target_pairs={{0,8},{1,3},{2,10},{3,5},{4,12},{5,7},{6,14},{7,1},{8,16},{9,11},{... | collective-permute-start | bytes 614408 | tf_op jit(solution)/shard_map/ppermute | solution.py:294
  2.2 2.7 %collective-permute-start.29 = (f32[400,128]{1,0:T(8,128)}, f32[400,128]{1,0:T(8,128)S(1)}, u32[]{:S(2)}, u32[]{:S(2)}) collective-permute-start(f32[400,128]{1,0:T(8,128)} %bitcast.25), channel_id=1, source_target_pairs={{0,16},{1,5},{2,18},{3,7},{4,20},{5,1},{6,22},{7,3},{8,24},{9,13},... | collective-permute-start | bytes 614408 | tf_op jit(solution)/shard_map/ppermute | solution.py:294
  4.9 1.4 %collective-permute-start.28 = (f32[400,128]{1,0:T(8,128)}, f32[400,128]{1,0:T(8,128)S(1)}, u32[]{:S(2)}, u32[]{:S(2)}) collective-permute-start(f32[400,128]{1,0:T(8,128)} %bitcast.26), channel_id=1, source_target_pairs={{0,24},{1,7},{2,26},{3,1},{4,28},{5,3},{6,30},{7,5},{8,0},{9,15},{... | collective-permute-start | bytes 614408 | tf_op jit(solution)/shard_map/ppermute | solution.py:294
  7.0 1.8 %pack.1 = (f32[456,128]{1,0:T(8,128)S(1)}, bf16[400,128]{1,0:T(8,128)(2,1)}, s32[32]{0:T(128)}) custom-call(s32[3]{0:T(128)} %pad_add_fusion.pos_ref, s32[1,32]{1,0:T(1,128)} %count_ref.1, s32[3]{0:T(128)} %neg_ref.1, f32[400,128]{1,0:T(8,128)} %bitcast.27, s32[12,128]{1,0:T(8,128)} %bitcast.28, s32[12,128]{1,0:T(8,128)} %bitcast.29, s32[12,128]{1,0:T(8,128)} %bitcast.30, ...), custom_call_target="tpu_custom_call" | custom-call | tf_op jit(solution)/shard_map/pack/pallas_call | solution.py:254
  8.8 2.2 %collective-permute-done.29 = f32[400,128]{1,0:T(8,128)S(1)} collective-permute-done((f32[400,128]{1,0:T(8,128)}, f32[400,128]{1,0:T(8,128)S(1)}, u32[]{:S(2)}, u32[]{:S(2)}) %collective-permute-start.29) | collective-permute-done | bytes 204832 | tf_op jit(solution)/shard_map/ppermute | solution.py:294
  11.1 1.9 %collective-permute-start.32 = (f32[4,400,128]{2,1,0:T(8,128)S(1)}, f32[4,400,128]{2,1,0:T(8,128)S(1)}, u32[]{:S(2)}, u32[]{:S(2)}) collective-permute-start(f32[4,400,128]{2,1,0:T(8,128)S(1)} %pad_maximum_fusion.7.refs_0_), channel_id=1, source_target_pairs={{0,2},{1,9},{2,4},{3,11},{4,6},{5,13},{6,0},{7,15},{8,10},{9,17},{... | collective-permute-start | bytes 2457608 | tf_op jit(solution)/shard_map/ppermute | solution.py:294
  13.9 16.0 %conditional.2 = (f32[456,128]{1,0:T(8,128)}) conditional(s32[]{:T(128)} %bitcast.7, f32[456,128]{1,0:T(8,128)S(1)} %get-tuple-element.80, f32[456,128]{1,0:T(8,128)S(1)} %get-tuple-element.80, f32[456,128]{1,0:T(8,128)S(1)} %get-tuple-element.80, f32[456,128]{1,0:T(8,128)S(1)} %get-tuple-element.80, ...), branch_computations={%region_0.1_spmd, %region_1.2_spmd, %region_2.3_spmd, %region_3.4_... | conditional | bytes 933936 | solution.py:306
  13.9 5.9 %collective-permute-start.6 = (f32[456,128]{1,0:T(8,128)S(1)}, f32[456,128]{1,0:T(8,128)}, u32[]{:S(2)}, u32[]{:S(2)}) collective-permute-start(f32[456,128]{1,0:T(8,128)S(1)} %param.6), channel_id=1, source_target_pairs={{0,224},{32,192},{64,160},{96,128},{128,96},{160,64},{192,32},{224... | collective-permute-start | bytes 700424 | tf_op jit(solution)/shard_map/cond/branch_6_fun/ppermute | solution.py:302
  19.9 10.0 %collective-permute-done.6 = f32[456,128]{1,0:T(8,128)} collective-permute-done((f32[456,128]{1,0:T(8,128)S(1)}, f32[456,128]{1,0:T(8,128)}, u32[]{:S(2)}, u32[]{:S(2)}) %collective-permute-start.6) | collective-permute-done | bytes 233504 | tf_op jit(solution)/shard_map/cond/branch_6_fun/ppermute | solution.py:302
  32.8 1.5 %collective-permute-start.33 = (f32[2,400,128]{2,1,0:T(8,128)S(1)}, f32[2,400,128]{2,1,0:T(8,128)S(1)}, u32[]{:S(2)}, u32[]{:S(2)}) collective-permute-start(f32[2,400,128]{2,1,0:T(8,128)S(1)} %get-tuple-element.91), channel_id=1, source_target_pairs={{0,2},{1,9},{2,4},{3,11},{4,6},{5,13},{6,0},{7,15},{8,10},{9,17},{... | collective-permute-start | bytes 1228808 | tf_op jit(solution)/shard_map/ppermute | solution.py:294
  34.3 5.9 %collective-permute-done.34.refs_4_ = f32[2,400,128]{2,1,0:T(8,128)S(1)} collective-permute-done((f32[2,400,128]{2,1,0:T(8,128)S(1)}, f32[2,400,128]{2,1,0:T(8,128)S(1)}, u32[]{:S(2)}, u32[]{:S(2)}) %collective-permute-start.34) | collective-permute-done | bytes 409632 | tf_op jit(solution)/shard_map/ppermute | solution.py:294
  42.6 16.6 %edges.1 = (f32[32,152,128]{2,1,0:T(8,128)}, f32[400,128]{1,0:T(8,128)S(1)}, f32[64,128]{1,0:T(8,128)S(1)}) custom-call(s32[32]{0:T(128)S(1)} %copy-done.1, f32[456,128]{1,0:T(8,128)} %get-tuple-element.151.z_ref, bf16[400,128]{1,0:T(8,128)(2,1)S(1)} %copy-done, f32[4,400,128]{2,1,0:T(8,128)S(1)} %pad_maximum_fusion.7.refs_0_, ...), custom_call_target="tpu_custom_call" | custom-call | flops 12000000000 | bytes 14000000 | tf_op jit(solution)/shard_map/edges/pallas_call | solution.py:191
  59.2 6.4 %all-to-all-start = ((f32[32,152,128]{2,1,0:T(8,128)}), f32[32,152,128]{2,1,0:T(8,128)S(1)}, u32[]{:S(2)}, u32[]{:S(2)}) async-start(f32[32,152,128]{2,1,0:T(8,128)} %get-tuple-element.82), calls=%async_computation | async-start | bytes 4980736 | tf_op jit(solution)/shard_map/all_to_all | solution.py:350
  65.6 22.9 %conditional.3 = (f32[464,128]{1,0:T(8,128)}, f32[64,128]{1,0:T(8,128)}, f32[64,128]{1,0:T(8,128)S(1)}, f32[64,128]{1,0:T(8,128)}) conditional(s32[]{:T(128)} %bitcast.7, (f32[400,128]{1,0:T(8,128)S(1)}, f32[64,128]{1,0:T(8,128)S(1)}) %tuple.95, (f32[400,128]{1,0:T(8,128)S(1)}, f32[64,128]{1,0:T(8,128)S(1)}) %tuple.95, ...), branch_computations={%region_7.8_spmd, %region_8.9_spmd, %region_9.10_spmd, %region_10.... | conditional | flops 75776 | bytes 1949848 | solution.py:352
  65.7 3.0 %collective-permute-start.25 = (f32[464,128]{1,0:T(8,128)S(1)}, f32[464,128]{1,0:T(8,128)}, u32[]{:S(2)}, u32[]{:S(2)}) collective-permute-start(f32[464,128]{1,0:T(8,128)S(1)} %pad_maximum_fusion.6), channel_id=1, source_target_pairs={{0,224},{32,192},{64,160},{96,128},{128,96},{160,64},{192,32},{224... | collective-permute-start | bytes 712712 | tf_op jit(solution)/shard_map/cond/branch_6_fun/ppermute | solution.py:302
  68.7 9.4 %collective-permute-done.25 = f32[464,128]{1,0:T(8,128)} collective-permute-done((f32[464,128]{1,0:T(8,128)S(1)}, f32[464,128]{1,0:T(8,128)}, u32[]{:S(2)}, u32[]{:S(2)}) %collective-permute-start.25) | collective-permute-done | bytes 237600 | tf_op jit(solution)/shard_map/cond/branch_6_fun/ppermute | solution.py:302
  78.9 3.9 %collective-permute-done.26 = f32[64,128]{1,0:T(8,128)S(1)} collective-permute-done((f32[64,128]{1,0:T(8,128)S(1)}, f32[64,128]{1,0:T(8,128)S(1)}, u32[]{:S(2)}, u32[]{:S(2)}) %collective-permute-start.26) | collective-permute-done | bytes 32800 | tf_op jit(solution)/shard_map/cond/branch_6_fun/ppermute | solution.py:302
  84.6 3.9 %collective-permute-done.27 = f32[64,128]{1,0:T(8,128)} collective-permute-done((f32[64,128]{1,0:T(8,128)}, f32[64,128]{1,0:T(8,128)}, u32[]{:S(2)}, u32[]{:S(2)}) %collective-permute-start.27) | collective-permute-done | bytes 32800 | tf_op jit(solution)/shard_map/cond/branch_6_fun/ppermute | solution.py:302
  89.3 1.2 %collective-permute-done.40 = f32[64,128]{1,0:T(8,128)S(1)} collective-permute-done((f32[64,128]{1,0:T(8,128)S(1)}, f32[64,128]{1,0:T(8,128)S(1)}, u32[]{:S(2)}, u32[]{:S(2)}) %collective-permute-start.40) | collective-permute-done | bytes 32800 | tf_op jit(solution)/shard_map/ppermute | solution.py:325
  91.4 4.9 %collective-permute-done.41 = f32[64,128]{1,0:T(8,128)S(1)} collective-permute-done((f32[64,128]{1,0:T(8,128)S(1)}, f32[64,128]{1,0:T(8,128)S(1)}, u32[]{:S(2)}, u32[]{:S(2)}) %collective-permute-start.41) | collective-permute-done | bytes 32800 | tf_op jit(solution)/shard_map/ppermute | solution.py:325
  96.3 5.1 %collective-permute-done.42 = f32[64,128]{1,0:T(8,128)S(1)} collective-permute-done((f32[64,128]{1,0:T(8,128)S(1)}, f32[64,128]{1,0:T(8,128)S(1)}, u32[]{:S(2)}, u32[]{:S(2)}) %collective-permute-start.42) | collective-permute-done | bytes 32800 | tf_op jit(solution)/shard_map/ppermute | solution.py:325
  101.8 3.6 %collective-permute-done.43 = f32[64,128]{1,0:T(8,128)S(1)} collective-permute-done((f32[64,128]{1,0:T(8,128)S(1)}, f32[64,128]{1,0:T(8,128)S(1)}, u32[]{:S(2)}, u32[]{:S(2)}) %collective-permute-start.43) | collective-permute-done | bytes 32800 | tf_op jit(solution)/shard_map/ppermute | solution.py:325
  105.4 1.8 %collective-permute-start.44 = (f32[64,128]{1,0:T(8,128)S(1)}, f32[64,128]{1,0:T(8,128)S(1)}, u32[]{:S(2)}, u32[]{:S(2)}) collective-permute-start(f32[64,128]{1,0:T(8,128)S(1)} %fusion.3), channel_id=1, source_target_pairs={{0,24},{1,25},{2,26},{3,27},{4,28},{5,29},{6,30},{7,31},{8,16},{9,... | collective-permute-start | bytes 98312 | tf_op jit(solution)/shard_map/ppermute | solution.py:325
  107.2 3.3 %last.1 = (f32[400,128]{1,0:T(8,128)}, f32[1,128]{1,0:T(1,128)}) custom-call(f32[32,152,128]{2,1,0:T(8,128)} %copy-done.2, f32[464,128]{1,0:T(8,128)} %get-tuple-element.85.lhs_ref, f32[1,128]{1,0:T(1,128)} %bitcast.32), custom_call_target="tpu_custom_call" | custom-call | tf_op jit(solution)/shard_map/last/pallas_call | solution.py:354
  (49 shorter events, 12.3 us)
Async XLA Ops:
  0.6 8.2 %collective-permute-start.30 = (f32[400,128]{1,0:T(8,128)}, f32[400,128]{1,0:T(8,128)S(1)}, u32[]{:S(2)}, u32[]{:S(2)}) collective-permute-start(f32[400,128]{1,0:T(8,128)} %bitcast.24), channel_id=1, source_target_pairs={{0,8},{1,3},{2,10},{3,5},{4,12},{5,7},{6,14},{7,1},{8,16},{9,11},{... | collective-permute-start | bytes 614408 | tf_op jit(solution)/shard_map/ppermute | solution.py:294
  2.2 8.9 %collective-permute-start.29 = (f32[400,128]{1,0:T(8,128)}, f32[400,128]{1,0:T(8,128)S(1)}, u32[]{:S(2)}, u32[]{:S(2)}) collective-permute-start(f32[400,128]{1,0:T(8,128)} %bitcast.25), channel_id=1, source_target_pairs={{0,16},{1,5},{2,18},{3,7},{4,20},{5,1},{6,22},{7,3},{8,24},{9,13},... | collective-permute-start | bytes 614408 | tf_op jit(solution)/shard_map/ppermute | solution.py:294
  4.9 6.1 %collective-permute-start.28 = (f32[400,128]{1,0:T(8,128)}, f32[400,128]{1,0:T(8,128)S(1)}, u32[]{:S(2)}, u32[]{:S(2)}) collective-permute-start(f32[400,128]{1,0:T(8,128)} %bitcast.26), channel_id=1, source_target_pairs={{0,24},{1,7},{2,26},{3,1},{4,28},{5,3},{6,30},{7,5},{8,0},{9,15},{... | collective-permute-start | bytes 614408 | tf_op jit(solution)/shard_map/ppermute | solution.py:294
  8.8 33.8 %copy-start = (bf16[400,128]{1,0:T(8,128)(2,1)S(1)}, bf16[400,128]{1,0:T(8,128)(2,1)}, u32[]{:S(2)}) copy-start(bf16[400,128]{1,0:T(8,128)(2,1)} %get-tuple-element.81.rel_ref) | copy-start | bytes 307204
  8.8 33.8 %copy-start.1 = (s32[32]{0:T(128)S(1)}, s32[32]{0:T(128)}, u32[]{:S(2)}) copy-start(s32[32]{0:T(128)} %get-tuple-element.79.slot_ref) | copy-start | bytes 388
  11.1 19.8 %collective-permute-start.32 = (f32[4,400,128]{2,1,0:T(8,128)S(1)}, f32[4,400,128]{2,1,0:T(8,128)S(1)}, u32[]{:S(2)}, u32[]{:S(2)}) collective-permute-start(f32[4,400,128]{2,1,0:T(8,128)S(1)} %pad_maximum_fusion.7.refs_0_), channel_id=1, source_target_pairs={{0,2},{1,9},{2,4},{3,11},{4,6},{5,13},{6,0},{7,15},{8,10},{9,17},{... | collective-permute-start | bytes 2457608 | tf_op jit(solution)/shard_map/ppermute | solution.py:294
  13.1 17.9 %collective-permute-start.31 = (f32[4,400,128]{2,1,0:T(8,128)S(1)}, f32[4,400,128]{2,1,0:T(8,128)S(1)}, u32[]{:S(2)}, u32[]{:S(2)}) collective-permute-start(f32[4,400,128]{2,1,0:T(8,128)S(1)} %pad_maximum_fusion.7.refs_0_), channel_id=1, source_target_pairs={{0,6},{1,25},{2,0},{3,27},{4,2},{5,29},{6,4},{7,31},{8,14},{9,1},{... | collective-permute-start | bytes 2457608 | tf_op jit(solution)/shard_map/ppermute | solution.py:294
  13.9 15.9 %collective-permute-start.6 = (f32[456,128]{1,0:T(8,128)S(1)}, f32[456,128]{1,0:T(8,128)}, u32[]{:S(2)}, u32[]{:S(2)}) collective-permute-start(f32[456,128]{1,0:T(8,128)S(1)} %param.6), channel_id=1, source_target_pairs={{0,224},{32,192},{64,160},{96,128},{128,96},{160,64},{192,32},{224... | collective-permute-start | bytes 700424 | tf_op jit(solution)/shard_map/cond/branch_6_fun/ppermute | solution.py:302
  30.8 10.0 %collective-permute-start.35 = (f32[4,400,128]{2,1,0:T(8,128)S(1)}, f32[4,400,128]{2,1,0:T(8,128)S(1)}, u32[]{:S(2)}, u32[]{:S(2)}) collective-permute-start(f32[4,400,128]{2,1,0:T(8,128)S(1)} %pad_maximum_fusion.7.refs_0_), channel_id=1, source_target_pairs={{0,1},{1,0},{2,3},{3,2},{4,5},{5,4},{6,7},{7,6},{8,9},{9,8},{10,11... | collective-permute-start | bytes 2457608 | tf_op jit(solution)/shard_map/ppermute | solution.py:298
  31.0 9.2 %collective-permute-start.34 = (f32[2,400,128]{2,1,0:T(8,128)S(1)}, f32[2,400,128]{2,1,0:T(8,128)S(1)}, u32[]{:S(2)}, u32[]{:S(2)}) collective-permute-start(f32[2,400,128]{2,1,0:T(8,128)S(1)} %get-tuple-element.90), channel_id=1, source_target_pairs={{0,6},{1,25},{2,0},{3,27},{4,2},{5,29},{6,4},{7,31},{8,14},{9,1},{... | collective-permute-start | bytes 1228808 | tf_op jit(solution)/shard_map/ppermute | solution.py:294
  32.1 8.8 %collective-permute-start.37 = (f32[4,400,128]{2,1,0:T(8,128)S(1)}, f32[4,400,128]{2,1,0:T(8,128)S(1)}, u32[]{:S(2)}, u32[]{:S(2)}) collective-permute-start(f32[4,400,128]{2,1,0:T(8,128)S(1)} %collective-permute-done.32.refs_2_), channel_id=1, source_target_pairs={{0,1},{1,0},{2,3},{3,2},{4,5},{5,4},{6,7},{7,6},{8,9},{9,8},{10,11... | collective-permute-start | bytes 2457608 | tf_op jit(solution)/shard_map/ppermute | solution.py:298
  32.8 8.0 %collective-permute-start.33 = (f32[2,400,128]{2,1,0:T(8,128)S(1)}, f32[2,400,128]{2,1,0:T(8,128)S(1)}, u32[]{:S(2)}, u32[]{:S(2)}) collective-permute-start(f32[2,400,128]{2,1,0:T(8,128)S(1)} %get-tuple-element.91), channel_id=1, source_target_pairs={{0,2},{1,9},{2,4},{3,11},{4,6},{5,13},{6,0},{7,15},{8,10},{9,17},{... | collective-permute-start | bytes 1228808 | tf_op jit(solution)/shard_map/ppermute | solution.py:294
  34.3 8.3 %collective-permute-start.36 = (f32[4,400,128]{2,1,0:T(8,128)S(1)}, f32[4,400,128]{2,1,0:T(8,128)S(1)}, u32[]{:S(2)}, u32[]{:S(2)}) collective-permute-start(f32[4,400,128]{2,1,0:T(8,128)S(1)} %collective-permute-done.31.refs_1_), channel_id=1, source_target_pairs={{0,1},{1,0},{2,3},{3,2},{4,5},{5,4},{6,7},{7,6},{8,9},{9,8},{10,11... | collective-permute-start | bytes 2457608 | tf_op jit(solution)/shard_map/ppermute | solution.py:298
  40.2 1.7 %collective-permute-start.39 = (f32[2,400,128]{2,1,0:T(8,128)S(1)}, f32[2,400,128]{2,1,0:T(8,128)S(1)}, u32[]{:S(2)}, u32[]{:S(2)}) collective-permute-start(f32[2,400,128]{2,1,0:T(8,128)S(1)} %collective-permute-done.34.refs_4_), channel_id=1, source_target_pairs={{0,1},{1,0},{2,3},{3,2},{4,5},{5,4},{6,7},{7,6},{8,9},{9,8},{10,11... | collective-permute-start | bytes 1228808 | tf_op jit(solution)/shard_map/ppermute | solution.py:298
  40.8 1.8 %collective-permute-start.38 = (f32[2,400,128]{2,1,0:T(8,128)S(1)}, f32[2,400,128]{2,1,0:T(8,128)S(1)}, u32[]{:S(2)}, u32[]{:S(2)}) collective-permute-start(f32[2,400,128]{2,1,0:T(8,128)S(1)} %collective-permute-done.33.refs_3_), channel_id=1, source_target_pairs={{0,1},{1,0},{2,3},{3,2},{4,5},{5,4},{6,7},{7,6},{8,9},{9,8},{10,11... | collective-permute-start | bytes 1228808 | tf_op jit(solution)/shard_map/ppermute | solution.py:298
  59.2 46.2 %all-to-all-start = ((f32[32,152,128]{2,1,0:T(8,128)}), f32[32,152,128]{2,1,0:T(8,128)S(1)}, u32[]{:S(2)}, u32[]{:S(2)}) async-start(f32[32,152,128]{2,1,0:T(8,128)} %get-tuple-element.82), calls=%async_computation | async-start | bytes 4980736 | tf_op jit(solution)/shard_map/all_to_all | solution.py:350
  65.7 12.4 %collective-permute-start.25 = (f32[464,128]{1,0:T(8,128)S(1)}, f32[464,128]{1,0:T(8,128)}, u32[]{:S(2)}, u32[]{:S(2)}) collective-permute-start(f32[464,128]{1,0:T(8,128)S(1)} %pad_maximum_fusion.6), channel_id=1, source_target_pairs={{0,224},{32,192},{64,160},{96,128},{128,96},{160,64},{192,32},{224... | collective-permute-start | bytes 712712 | tf_op jit(solution)/shard_map/cond/branch_6_fun/ppermute | solution.py:302
  78.9 3.9 %collective-permute-start.26 = (f32[64,128]{1,0:T(8,128)S(1)}, f32[64,128]{1,0:T(8,128)S(1)}, u32[]{:S(2)}, u32[]{:S(2)}) collective-permute-start(f32[64,128]{1,0:T(8,128)S(1)} %slice_add_fusion.6), channel_id=1, source_target_pairs={{0,32},{32,0},{64,96},{96,64},{128,160},{160,128},{192,224},{224,1... | collective-permute-start | bytes 98312 | tf_op jit(solution)/shard_map/cond/branch_6_fun/ppermute | solution.py:302
  83.4 5.1 %collective-permute-start.27 = (f32[64,128]{1,0:T(8,128)}, f32[64,128]{1,0:T(8,128)}, u32[]{:S(2)}, u32[]{:S(2)}) collective-permute-start(f32[64,128]{1,0:T(8,128)} %add.84), channel_id=1, source_target_pairs={{0,64},{32,96},{64,0},{96,32},{128,192},{160,224},{192,128},{224,1... | collective-permute-start | bytes 98312 | tf_op jit(solution)/shard_map/cond/branch_6_fun/ppermute | solution.py:302
  89.3 1.2 %collective-permute-start.40 = (f32[64,128]{1,0:T(8,128)S(1)}, f32[64,128]{1,0:T(8,128)S(1)}, u32[]{:S(2)}, u32[]{:S(2)}) collective-permute-start(f32[64,128]{1,0:T(8,128)S(1)} %add.103), channel_id=1, source_target_pairs={{0,1},{1,0},{2,3},{3,2},{4,5},{5,4},{6,7},{7,6},{8,9},{9,8},{10,11... | collective-permute-start | bytes 98312 | tf_op jit(solution)/shard_map/ppermute | solution.py:325
  90.5 5.8 %collective-permute-start.41 = (f32[64,128]{1,0:T(8,128)S(1)}, f32[64,128]{1,0:T(8,128)S(1)}, u32[]{:S(2)}, u32[]{:S(2)}) collective-permute-start(f32[64,128]{1,0:T(8,128)S(1)} %add.104), channel_id=1, source_target_pairs={{0,2},{1,3},{2,0},{3,1},{4,6},{5,7},{6,4},{7,5},{8,10},{9,11},{10,... | collective-permute-start | bytes 98312 | tf_op jit(solution)/shard_map/ppermute | solution.py:325
  96.3 5.1 %collective-permute-start.42 = (f32[64,128]{1,0:T(8,128)S(1)}, f32[64,128]{1,0:T(8,128)S(1)}, u32[]{:S(2)}, u32[]{:S(2)}) collective-permute-start(f32[64,128]{1,0:T(8,128)S(1)} %add.105), channel_id=1, source_target_pairs={{0,6},{1,7},{2,4},{3,5},{4,2},{5,3},{6,0},{7,1},{8,14},{9,15},{10,... | collective-permute-start | bytes 98312 | tf_op jit(solution)/shard_map/ppermute | solution.py:325
  101.5 3.9 %collective-permute-start.43 = (f32[64,128]{1,0:T(8,128)S(1)}, f32[64,128]{1,0:T(8,128)S(1)}, u32[]{:S(2)}, u32[]{:S(2)}) collective-permute-start(f32[64,128]{1,0:T(8,128)S(1)} %add.106), channel_id=1, source_target_pairs={{0,8},{1,9},{2,10},{3,11},{4,12},{5,13},{6,14},{7,15},{8,0},{9,1},... | collective-permute-start | bytes 98312 | tf_op jit(solution)/shard_map/ppermute | solution.py:325
  105.4 5.2 %collective-permute-start.44 = (f32[64,128]{1,0:T(8,128)S(1)}, f32[64,128]{1,0:T(8,128)S(1)}, u32[]{:S(2)}, u32[]{:S(2)}) collective-permute-start(f32[64,128]{1,0:T(8,128)S(1)} %fusion.3), channel_id=1, source_target_pairs={{0,24},{1,25},{2,26},{3,27},{4,28},{5,29},{6,30},{7,31},{8,16},{9,... | collective-permute-start | bytes 98312 | tf_op jit(solution)/shard_map/ppermute | solution.py:325
  (1 other events, 1.8 us)
